TPU v7x, 32 devices: a whole 2x2x4 slice. The times are simulated.
32 devices in a mesh: tile: 16 (over z, y, x), rep: 2 (over core).
Axes of the slice: x: 2, y: 2, z: 4, core: 2. Of those that a mesh axis runs over, the one named last changes fastest.
Arguments:
- feats: bfloat16 [2, 128, 32768], P('rep', None, 'tile'), may hold values from -6 to 6
- coords: bfloat16 [2, 3, 32768], P('rep', None, 'tile'), may hold values from -2 to 2
- nbr_fine: int32 [2, 32, 32768], P('rep', None, 'tile'), may hold values from -1 to 1024, as said below
- counts: int32 [2, 16], P('rep', 'tile'), may hold values from 256 to 2048, as said below
- sub_index: int32 [2, 8192], P('rep', 'tile'), may hold values from 0 to 32767, as said below
- nbr_coarse: int32 [2, 32, 8192], P('rep', None, 'tile'), may hold values from -1 to 1024, as said below
- kernel_points: float32 [3, 15], replicated, may hold values from -2 to 2
- w_fine: bfloat16 [15, 128, 128], replicated, may hold values from -1.25 to 1.25
- w_coarse: bfloat16 [15, 128, 256], replicated, may hold values from -1.25 to 1.25
- grad_out: bfloat16 [2, 256, 8192], P('rep', None, 'tile'), may hold values from -6 to 6
Outputs:
- coarse_out: bfloat16 [2, 256, 8192], P('rep', None, 'tile')
- grad_wb: float32 [15, 128, 256], replicated
Inputs may be any that keep to these rules, and one draw needn't show every extreme that they name: `nbr_fine`: every neighbour slot that an entry names lies in the scan section; slots that are not valid have only -1 entries; every valid point has 8 to 32 filled entries, first in its list; some entry is 0 and some is 1024. `counts`: every scan section has one tile whose count is 2048. `sub_index`: subsampled point c sits in tile c div 512, at a valid slot. `nbr_coarse`: every neighbour slot that an entry names lies in the scan section; every subsampled point has 8 to 32 filled entries, first in its list.
All inputs are finite; a program needn't handle non-finite values.
Results may differ from a plain program's by a relative error of at most 0.0071.
Values may be sent and summed in bfloat16 or wider, within the bound.
A program may use at most 64 MiB of HBM per device.

v0:
```python
import math

import jax
import jax.numpy as jnp
from jax import lax
from jax.sharding import PartitionSpec as P

HALO = 512


kernel_sigma = 2.0
leak_slope = 0.1


def with_halo(cells, sides, width):
    for axis, dim in sides:
        count = lax.axis_size(axis)
        ends = count - 1
        head = lax.slice_in_dim(cells, 0, width, axis=dim)
        tail = lax.slice_in_dim(cells, cells.shape[dim] - width, cells.shape[dim], axis=dim)
        cells = jnp.concatenate(
            [
                lax.ppermute(tail, axis, [(i, (i + 1) % count) for i in range(ends)]),
                cells,
                lax.ppermute(head, axis, [((i + 1) % count, i) for i in range(ends)]),
            ],
            axis=dim,
        )
    return cells


def block_size():
    return 512


def absolute(offsets, base, reach):
    return jnp.where(offsets >= 0, base[None, :] + offsets - reach, -1)


def conv_block(source, place_src, indices, centre, first_row, kernel_points, weight_mat):
    present = indices >= 0
    local_rows = jnp.clip(indices - first_row, 0, source.shape[1] - 1)
    near_feat = jnp.take(source, local_rows, axis=1, mode="clip")
    near_pos = jnp.take(place_src, local_rows, axis=1, mode="clip").astype(jnp.float32)
    offsets = near_pos - centre[:, None, :]
    apart = offsets[:, None, :, :] - kernel_points[:, :, None, None]
    length = jnp.sqrt(jnp.sum(apart * apart, axis=0))
    weights = (
        jnp.maximum(1.0 - length / kernel_sigma, 0.0) * present.astype(jnp.float32)[None]
    ).astype(jnp.bfloat16)
    summed = jnp.einsum(
        "kjb,cjb->kcb", weights, near_feat, preferred_element_type=jnp.float32
    ).astype(jnp.bfloat16)
    flat = summed.reshape(-1, summed.shape[2])
    preact = lax.dot_general(
        weight_mat, flat, (((0,), (0,)), ((), ())), preferred_element_type=jnp.float32
    )
    return (preact, flat)


def run_rows(source, place_src, indices, centres, first_row, kernel_points, weight_mat):
    count = indices.shape[1]
    block_rows = block_size()

    def one_block(number, buffer):
        start = number * block_rows
        index_block = lax.dynamic_slice_in_dim(indices, start, block_rows, 1)
        centre_block = lax.dynamic_slice_in_dim(centres, start, block_rows, 1)
        preact, flat = conv_block(
            source, place_src, index_block, centre_block, first_row, kernel_points, weight_mat
        )
        result = jax.nn.leaky_relu(preact, leak_slope).astype(jnp.bfloat16)
        return lax.dynamic_update_slice_in_dim(buffer, result, start, 1)

    empty = jnp.zeros((weight_mat.shape[1], count), jnp.bfloat16)
    return lax.fori_loop(0, count // block_rows, one_block, empty)


def shards(
    feats,
    coords,
    nbr_fine,
    counts,
    sub_index,
    nbr_coarse,
    kernel_points,
    w_fine,
    w_coarse,
    grad_out,
):
    points = feats.shape[2]
    coarse = sub_index.shape[1]
    tile_index = lax.axis_index("tile")
    anchor = tile_index * points
    filled = counts[0, 0]
    rows_here = jnp.arange(points)
    valid = (rows_here < (filled + 1) // 2) | (rows_here >= points - filled // 2)
    masked = feats[0] * valid.astype(jnp.bfloat16)[None, :]
    places = coords[0]
    wide_a = w_fine.reshape(-1, w_fine.shape[2])
    wide_b = w_coarse.reshape(-1, w_coarse.shape[2])
    feat_ext, place_ext = (
        with_halo(masked, (("tile", 1),), HALO),
        with_halo(places, (("tile", 1),), HALO),
    )
    own_slots = anchor + jnp.arange(points, dtype=jnp.int32)
    fine_lists = absolute(nbr_fine[0], own_slots, HALO)
    hidden = run_rows(
        feat_ext,
        place_ext,
        fine_lists,
        places.astype(jnp.float32),
        anchor - HALO,
        kernel_points,
        wide_a,
    )
    hidden_ext = with_halo(hidden, (("tile", 1),), HALO)
    centres = jnp.take(places.astype(jnp.float32), sub_index[0] - anchor, axis=1, mode="clip")
    block_rows = block_size()
    upstream_all = grad_out[0]
    indices_all = absolute(nbr_coarse[0], sub_index[0], HALO)

    def coarse_step(number, carry):
        buffer, grad_part = carry
        preact, flat = conv_block(
            hidden_ext, place_ext, indices_all, centres, anchor - HALO, kernel_points, wide_b
        )
        term = lax.dot_general(
            flat, upstream_all, (((1,), (1,)), ((), ())), preferred_element_type=jnp.float32
        )
        buffer = preact.astype(jnp.bfloat16)
        return (buffer, grad_part + term)

    start_carry = (
        jnp.zeros((wide_b.shape[1], coarse), jnp.bfloat16),
        jnp.zeros((wide_b.shape[0], wide_b.shape[1]), jnp.float32),
    )
    coarse_out, grad_part = lax.fori_loop(0, coarse // block_rows, coarse_step, start_carry)
    grad_total = lax.psum(grad_part, ("tile", "rep"))
    scale = 1.0 / math.sqrt(lax.axis_size("tile") * lax.axis_size("rep") * coarse)
    grad_wb = (grad_total * scale).reshape(w_coarse.shape)
    return (coarse_out[None], grad_wb)


def solution(mesh):
    placed = (
        P("rep", None, "tile"),
        P("rep", None, "tile"),
        P("rep", None, "tile"),
        P("rep", "tile"),
        P("rep", "tile"),
        P("rep", None, "tile"),
        P(),
        P(),
        P(),
        P("rep", None, "tile"),
    )
    return jax.shard_map(
        shards, mesh=mesh, in_specs=placed, out_specs=(P("rep", None, "tile"), P()), check_vma=False
    )
```

profile of v0, /device:TPU:3, one launch (start us, length us, event | category | flops | bytes accessed | tf_op | source)
XLA Modules:
  0.0 909.9 jit_solution(2759649163099932824)
XLA Ops:
  10.4 3.1 collective-permute-start
  13.6 2.8 collective-permute-start.1
  17.4 3.4 collective-permute-start.2
  25.6 2.1 collective-permute-done.3
  28.9 57.4 %gather_fusion.3 = bf16[16384,3]{1,0:T(8,128)(2,1)} fusion(bf16[3,3072]{0,1:T(8,128)(2,1)S(1)} %pad_maximum_fusion.1, s32[16384]{0:T(1024)S(1)} %broadcast_clamp_fusion.1), kind=kCustom, calls=%fused_computation.3 | custom fusion | bytes 262144 | tf_op jit(solution)/shard_map/while/body/eval_jaxpr/jit(_take)/gather | solution.py:44
  86.3 6.4 fusion.8
  92.7 5.2 copy.58
  101.3 580.9 %while.8 = (s32[]{:T(128)}, bf16[128,2048]{0,1:T(8,128)(2,1)}, s32[32,2048]{1,0:T(8,128)S(1)}, s32[]{:T(128)}, bf16[128,3072]{0,1:T(8,128)(2,1)S(1)}, /*index=5*...) while((s32[]{:T(128)}, bf16[128,2048]{0,1:T(8,128)(2,1)}, ...), condition=%wide.region_2.3_spmd, body=%wide.region_0.2_spmd.sunk | while | flops 319193088 | bytes 28789136 | solution.py:76
  101.4 57.4 %gather_fusion = bf16[16384,3]{1,0:T(8,128)(2,1)} fusion(bf16[3,3072]{0,1:T(8,128)(2,1)S(1)} %get-tuple-element.316, s32[16384]{0:T(1024)S(1)} %broadcast_clamp_fusion.3), kind=kCustom, calls=%fused_computation.1.clone.1 | custom fusion | bytes 262144 | tf_op jit(solution)/shard_map/while/body/eval_jaxpr/jit(_take)/gather | solution.py:44
  159.7 6.4 fusion.47
  166.2 5.2 copy.84
  172.2 2.8 copy.85
  175.0 57.4 %gather_fusion.1 = bf16[16384,128]{1,0:T(8,128)(2,1)} fusion(bf16[128,3072]{0,1:T(8,128)(2,1)S(1)} %get-tuple-element.315, s32[16384]{0:T(1024)S(1)} %broadcast_clamp_fusion.3), kind=kCustom, calls=%fused_computation.clone.1 | custom fusion | bytes 8454144 | tf_op jit(solution)/shard_map/while/body/eval_jaxpr/jit(_take)/gather | solution.py:43
  232.4 6.7 convert_bitcast_fusion.6
  239.1 4.5 copy.86
  243.6 2.9 fusion.48
  246.6 57.4 %gather_fusion = bf16[16384,3]{1,0:T(8,128)(2,1)} fusion(bf16[3,3072]{0,1:T(8,128)(2,1)S(1)} %get-tuple-element.316, s32[16384]{0:T(1024)S(1)} %broadcast_clamp_fusion.3), kind=kCustom, calls=%fused_computation.1.clone.1 | custom fusion | bytes 262144 | tf_op jit(solution)/shard_map/while/body/eval_jaxpr/jit(_take)/gather | solution.py:44
  304.9 6.4 fusion.47
  311.4 5.2 copy.84
  317.4 2.8 copy.85
  320.2 57.4 %gather_fusion.1 = bf16[16384,128]{1,0:T(8,128)(2,1)} fusion(bf16[128,3072]{0,1:T(8,128)(2,1)S(1)} %get-tuple-element.315, s32[16384]{0:T(1024)S(1)} %broadcast_clamp_fusion.3), kind=kCustom, calls=%fused_computation.clone.1 | custom fusion | bytes 8454144 | tf_op jit(solution)/shard_map/while/body/eval_jaxpr/jit(_take)/gather | solution.py:43
  377.6 6.7 convert_bitcast_fusion.6
  384.3 4.5 copy.86
  388.8 2.9 fusion.48
  391.8 57.4 %gather_fusion = bf16[16384,3]{1,0:T(8,128)(2,1)} fusion(bf16[3,3072]{0,1:T(8,128)(2,1)S(1)} %get-tuple-element.316, s32[16384]{0:T(1024)S(1)} %broadcast_clamp_fusion.3), kind=kCustom, calls=%fused_computation.1.clone.1 | custom fusion | bytes 262144 | tf_op jit(solution)/shard_map/while/body/eval_jaxpr/jit(_take)/gather | solution.py:44
  450.2 6.4 fusion.47
  456.6 5.2 copy.84
  462.6 2.8 copy.85
  465.4 57.4 %gather_fusion.1 = bf16[16384,128]{1,0:T(8,128)(2,1)} fusion(bf16[128,3072]{0,1:T(8,128)(2,1)S(1)} %get-tuple-element.315, s32[16384]{0:T(1024)S(1)} %broadcast_clamp_fusion.3), kind=kCustom, calls=%fused_computation.clone.1 | custom fusion | bytes 8454144 | tf_op jit(solution)/shard_map/while/body/eval_jaxpr/jit(_take)/gather | solution.py:43
  522.8 6.7 convert_bitcast_fusion.6
  529.5 4.5 copy.86
  534.1 2.9 fusion.48
  537.0 57.4 %gather_fusion = bf16[16384,3]{1,0:T(8,128)(2,1)} fusion(bf16[3,3072]{0,1:T(8,128)(2,1)S(1)} %get-tuple-element.316, s32[16384]{0:T(1024)S(1)} %broadcast_clamp_fusion.3), kind=kCustom, calls=%fused_computation.1.clone.1 | custom fusion | bytes 262144 | tf_op jit(solution)/shard_map/while/body/eval_jaxpr/jit(_take)/gather | solution.py:44
  595.4 6.4 fusion.47
  601.8 5.2 copy.84
  607.8 2.8 copy.85
  610.6 57.4 %gather_fusion.1 = bf16[16384,128]{1,0:T(8,128)(2,1)} fusion(bf16[128,3072]{0,1:T(8,128)(2,1)S(1)} %get-tuple-element.315, s32[16384]{0:T(1024)S(1)} %broadcast_clamp_fusion.3), kind=kCustom, calls=%fused_computation.clone.1 | custom fusion | bytes 8454144 | tf_op jit(solution)/shard_map/while/body/eval_jaxpr/jit(_take)/gather | solution.py:43
  668.0 6.7 convert_bitcast_fusion.6
  674.7 4.5 copy.86
  679.3 2.9 fusion.48
  683.2 3.2 collective-permute-start.4
  686.4 2.4 collective-permute-start.5
  690.4 2.8 copy.59
  693.9 57.4 %gather_fusion.2 = bf16[16384,128]{1,0:T(8,128)(2,1)} fusion(bf16[128,3072]{0,1:T(8,128)(2,1)S(1)} %pad_maximum_fusion.2, s32[16384]{0:T(1024)S(1)} %broadcast_clamp_fusion.1), kind=kCustom, calls=%fused_computation.2 | custom fusion | bytes 8454144 | tf_op jit(solution)/shard_map/while/body/eval_jaxpr/jit(_take)/gather | solution.py:43
  751.3 6.7 convert_bitcast_fusion.3
  758.1 3.5 copy.61
  765.2 134.9 %all-reduce.2.cloned.1.call-done = f32[1920,256]{1,0:T(8,128)} async-done(((f32[1920,256]{1,0:T(8,128)}), f32[1920,256]{1,0:T(8,128)}) %all-reduce.2.cloned.1.call-update) | async-done | bytes 1966096 | tf_op jit(solution)/shard_map/psum | solution.py:139
  900.1 2.9 broadcast_multiply_fusion
  (94 shorter events, 26.5 us)
Async XLA Ops:
  7.2 756.5 %copy-start = (bf16[15,128,256]{2,1,0:T(8,128)(2,1)S(1)}, bf16[15,128,256]{2,1,0:T(8,128)(2,1)}, u32[]{:S(2)}) copy-start(bf16[15,128,256]{2,1,0:T(8,128)(2,1)} %param.20) | copy-start | bytes 2949124
  7.2 9.2 %copy-start.11 = (bf16[1,3,2048]{2,1,0:T(4,128)(2,1)S(1)}, bf16[1,3,2048]{2,1,0:T(4,128)(2,1)}, u32[]{:S(2)}) copy-start(bf16[1,3,2048]{2,1,0:T(4,128)(2,1)} %param.13) | copy-start | bytes 36868
  7.2 892.9 %all-reduce.2.cloned.1.call-start = ((), (), s32[]{:S(2)}) async-start(), calls=%async_computation | async-start | bytes 3932160 | tf_op jit(solution)/shard_map/psum | solution.py:139
  9.3 13.5 %copy-start.10 = (s32[1,512]{1,0:T(1,128)S(1)}, s32[1,512]{1,0:T(1,128)}, u32[]{:S(2)}) copy-start(s32[1,512]{1,0:T(1,128)} %param.16) | copy-start | bytes 6148
  9.4 13.5 %copy-start.6 = (s32[1,32,512]{2,1,0:T(8,128)S(1)}, s32[1,32,512]{2,1,0:T(8,128)}, u32[]{:S(2)}) copy-start(s32[1,32,512]{2,1,0:T(8,128)} %param.17) | copy-start | bytes 196612
  9.7 3.9 copy-start.2
  9.7 13.3 %copy-start.5 = (s32[1,32,2048]{2,1,0:T(8,128)S(1)}, s32[1,32,2048]{2,1,0:T(8,128)}, u32[]{:S(2)}) copy-start(s32[1,32,2048]{2,1,0:T(8,128)} %param.14) | copy-start | bytes 786436
  10.4 88.8 %collective-permute-start = (bf16[128,512]{0,1:T(8,128)(2,1)}, bf16[128,512]{0,1:T(8,128)(2,1)}, u32[]{:S(2)}, u32[]{:S(2)}) collective-permute-start(bf16[128,512]{0,1:T(8,128)(2,1)} %get-tuple-element.226), channel_id=1, source_target_pairs={{0,2},{2,4},{4,6},{6,8},{8,10},{10,12},{12,14},{14,16},{16,18},{18... | collective-permute-start | bytes 393224 | tf_op jit(solution)/shard_map/ppermute | solution.py:23
  13.6 85.7 %collective-permute-start.1 = (bf16[128,512]{0,1:T(8,128)(2,1)}, bf16[128,512]{0,1:T(8,128)(2,1)}, u32[]{:S(2)}, u32[]{:S(2)}) collective-permute-start(bf16[128,512]{0,1:T(8,128)(2,1)} %get-tuple-element.227), channel_id=1, source_target_pairs={{2,0},{4,2},{6,4},{8,6},{10,8},{12,10},{14,12},{16,14},{18,16},{20... | collective-permute-start | bytes 393224 | tf_op jit(solution)/shard_map/ppermute | solution.py:25
  17.4 7.5 collective-permute-start.2
  20.8 6.9 collective-permute-start.3
  22.8 2.1 copy-start.1
  24.9 0.7 copy-start.8
  27.7 58.5 %copy-start.4 = (f32[512,3]{1,0:T(8,128)S(1)}, f32[512,3]{1,0:T(8,128)}, u32[]{:S(2)}) copy-start(f32[512,3]{1,0:T(8,128)} %gather_fusion.4) | copy-start | bytes 18436
  92.7 5.2 copy-start.9
  239.1 4.5 copy-start.12
  384.3 4.5 copy-start.12
  529.5 4.5 copy-start.12
  674.7 4.5 copy-start.12
  683.2 10.7 %copy-start.3 = (bf16[128,2048]{0,1:T(8,128)(2,1)S(1)}, bf16[128,2048]{0,1:T(8,128)(2,1)}, u32[]{:S(2)}) copy-start(bf16[128,2048]{0,1:T(8,128)(2,1)} %get-tuple-element.188) | copy-start | bytes 1572868
  683.2 10.0 %collective-permute-start.4 = (bf16[128,512]{0,1:T(8,128)(2,1)S(1)}, bf16[128,512]{0,1:T(8,128)(2,1)S(1)}, u32[]{:S(2)}, u32[]{:S(2)}) collective-permute-start(bf16[128,512]{0,1:T(8,128)(2,1)S(1)} %get-tuple-element.224), channel_id=1, source_target_pairs={{0,2},{2,4},{4,6},{6,8},{8,10},{10,12},{12,14},{14,16},{16,18},{18... | collective-permute-start | bytes 393224 | tf_op jit(solution)/shard_map/ppermute | solution.py:23
  686.4 7.5 collective-permute-start.5
  758.1 3.6 copy-start.7
Sparse Core Ops, SparseCore 0:
  763.7 136.3 all-reduce.1
where the time goes:
time: 914 us; the launch traced here: 910 us
  local copies, waits for them, and re-layouts  648 us (71%)
  waiting for transfers between devices  138 us (15%)
  matrix products  48.1 us (5%)
  other arithmetic  44 us (5%)
  starting transfers between devices  16.8 us (2%)
  between operations  15.1 us (2%)
    gather x5, local copies, waits for them, and re-layouts, conv_block(): near_feat = jnp.take(source, local_rows, axis=1, mode='clip')  287 us
    gather x5, local copies, waits for them, and re-layouts, conv_block(): jnp.take(place_src, local_rows, axis=1, mode='clip').astype(jnp.float32)  287 us
    psum x1, waiting for transfers between devices, shards(): grad_total = lax.psum(grad_part, ('tile', 'rep'))  135 us
    dot_general x5, matrix products, conv_block(): jnp.einsum('kjb,cjb->kcb', weights, near_feat, preferred_element_type=jnp...  33.7 us
    sub x5, other arithmetic, conv_block(): offsets = near_pos - centre[:, None, :]  32.2 us
    sub x5, local copies, waits for them, and re-layouts, conv_block(): offsets = near_pos - centre[:, None, :]  26.1 us
    convert_element_type x5, local copies, waits for them, and re-layouts, conv_block(): summed = jnp.einsum('kjb,cjb->kcb', weights, near_feat, preferred_element...  21.6 us
  transfers between devices with their start and end apart: 7, of which 4 were waited for; matrix products, arithmetic and copies ran while one was open for 9% of the time, Pallas kernels for 0%

commit v1 on v0

v1 whole, which is shorter than its diff:
```python
import functools
import math

import jax
import jax.numpy as jnp
from jax import lax
from jax.experimental import pallas as pl
from jax.experimental.pallas import tpu as pltpu
from jax.sharding import PartitionSpec as P

HALO = 512
GROUP = 8
LANES = 128

kernel_sigma = 2.0
leak_slope = 0.1


def with_halo(cells, axis, width, dim):
    count = lax.axis_size(axis)
    ends = count - 1
    head = lax.slice_in_dim(cells, 0, width, axis=dim)
    tail = lax.slice_in_dim(cells, cells.shape[dim] - width, cells.shape[dim], axis=dim)
    return jnp.concatenate(
        [
            lax.ppermute(tail, axis, [(i, (i + 1) % count) for i in range(ends)]),
            cells,
            lax.ppermute(head, axis, [((i + 1) % count, i) for i in range(ends)]),
        ],
        axis=dim,
    )


def conv_kernel(
    slots,
    kps,
    local,
    chunks,
    last,
    idx_s,
    idx_v,
    cen,
    kp,
    src,
    pos,
    *rest,
):
    if last:
        w, out, rows32, infl, g_even, g_odd, agg = rest
    else:
        out, rows32, infl, g_even, g_odd, agg = rest
    step = pl.program_id(0)
    blocks = idx_v.shape[0]
    width = GROUP * slots
    total = src.shape[0]

    @pl.when(step == 0)
    def _():
        rows32[...] = src[...].astype(jnp.float32)

    first_chunk = (step * blocks * GROUP) // LANES if local else 0
    for half in range(width // LANES):
        cols = slice(half * LANES, (half + 1) * LANES)
        idx = idx_v[:, cols]
        lane = jnp.bitwise_and(idx, LANES - 1)
        chunk = jnp.right_shift(idx, 7)
        near = [jnp.zeros(idx.shape, jnp.float32) for _ in range(3)]
        for c in range(chunks):
            here = chunk == first_chunk + c
            start = (first_chunk + c) * LANES
            if local:
                start = pl.multiple_of(start, LANES)
            for d in range(3):
                piece = jnp.broadcast_to(pos[d : d + 1, pl.ds(start, LANES)], idx.shape)
                got = jnp.take_along_axis(piece, lane, axis=1)
                near[d] = jnp.where(here, got, near[d])
        offs = [near[d] - cen[d, :, cols] for d in range(3)]
        present = idx >= 0
        for k in range(kps):
            a0 = offs[0] - kp[0, k]
            a1 = offs[1] - kp[1, k]
            a2 = offs[2] - kp[2, k]
            length = jnp.sqrt(a0 * a0 + a1 * a1 + a2 * a2)
            infl[k, :, cols] = jnp.where(
                present, jnp.maximum(1.0 - length / kernel_sigma, 0.0), 0.0
            )
    infl[kps] = jnp.zeros((blocks, width), jnp.float32)

    own = (
        lax.broadcasted_iota(jnp.int32, (GROUP, width), 1) // slots
        == lax.broadcasted_iota(jnp.int32, (GROUP, width), 0)
    )

    def fetch(block, g):
        base = block * width
        for r in range(width):
            row = idx_s[0, 0, base + r]
            g[r : r + 1, :] = rows32[pl.ds(row, 1), :]

    def combine(block, g):
        parts = []
        for k in range(kps + 1):
            one = jnp.broadcast_to(infl[k, pl.ds(block, 1), :], (GROUP, width))
            parts.append(jnp.where(own, one, 0.0))
        lhs = jnp.concatenate(parts, axis=0).astype(jnp.bfloat16)
        res = jnp.dot(lhs, g[...].astype(jnp.bfloat16), preferred_element_type=jnp.float32)
        at = pl.ds(pl.multiple_of(block * GROUP, GROUP), GROUP)
        for k in range(kps):
            agg[at, k * LANES : (k + 1) * LANES] = res[k * GROUP : (k + 1) * GROUP]

    fetch(0, g_even)

    def pair(p, carry):
        fetch(2 * p + 1, g_odd)
        combine(2 * p, g_even)
        fetch(jnp.minimum(2 * p + 2, blocks - 1), g_even)
        combine(2 * p + 1, g_odd)
        return carry

    lax.fori_loop(0, blocks // 2, pair, 0)
    flat = agg[...].astype(jnp.bfloat16)
    if last:
        pre = jnp.dot(flat, w[...], preferred_element_type=jnp.float32)
        out[...] = jnp.where(pre >= 0, pre, leak_slope * pre).astype(jnp.bfloat16)
    else:
        out[...] = flat


def conv(rows, place_ext, local_idx, centres, kernel_points, w, per_step, local):
    count, slots = local_idx.shape
    chans = rows.shape[1]
    kps = kernel_points.shape[1]
    total = rows.shape[0]
    per_step = min(per_step, count)
    steps = count // per_step
    blocks = per_step // GROUP
    width = GROUP * slots
    idx_s = jnp.maximum(local_idx, 0).reshape(steps, 1, per_step * slots)
    idx_v = local_idx.reshape(count // GROUP, width)
    cen = jnp.broadcast_to(centres[:, :, None], (3, count, slots)).reshape(3, count // GROUP, width)
    chunks = (per_step + 2 * HALO) // LANES if local else total // LANES
    last = w is not None
    outs = w.shape[1] if last else kps * chans
    in_specs = [
        pl.BlockSpec((1, 1, per_step * slots), lambda i: (i, 0, 0), memory_space=pltpu.SMEM),
        pl.BlockSpec((blocks, width), lambda i: (i, 0)),
        pl.BlockSpec((3, blocks, width), lambda i: (0, i, 0)),
        pl.BlockSpec(memory_space=pltpu.SMEM),
        pl.BlockSpec((total, chans), lambda i: (0, 0)),
        pl.BlockSpec(place_ext.shape, lambda i: (0, 0)),
    ]
    args = [idx_s, idx_v, cen, kernel_points, rows, place_ext]
    if last:
        in_specs.append(pl.BlockSpec(w.shape, lambda i: (0, 0)))
        args.append(w)
    return pl.pallas_call(
        functools.partial(conv_kernel, slots, kps, local, chunks, last),
        grid=(steps,),
        in_specs=in_specs,
        out_specs=pl.BlockSpec((per_step, outs), lambda i: (i, 0)),
        out_shape=jax.ShapeDtypeStruct((count, outs), jnp.bfloat16),
        scratch_shapes=[
            pltpu.VMEM((total, chans), jnp.float32),
            pltpu.VMEM((kps + 1, blocks, width), jnp.float32),
            pltpu.VMEM((width, chans), jnp.float32),
            pltpu.VMEM((width, chans), jnp.float32),
            pltpu.VMEM((per_step, kps * chans), jnp.float32),
        ],
        compiler_params=pltpu.CompilerParams(vmem_limit_bytes=40 * 1024 * 1024),
        name="fine_conv" if last else "coarse_agg",
    )(*args)


def shards(
    feats,
    coords,
    nbr_fine,
    counts,
    sub_index,
    nbr_coarse,
    kernel_points,
    w_fine,
    w_coarse,
    grad_out,
):
    points = feats.shape[2]
    coarse = sub_index.shape[1]
    anchor = lax.axis_index("tile") * points
    filled = counts[0, 0]
    rows_here = jnp.arange(points)
    valid = (rows_here < (filled + 1) // 2) | (rows_here >= points - filled // 2)
    masked = (feats[0] * valid.astype(jnp.bfloat16)[None, :]).T
    places = coords[0]
    wide_a = w_fine.reshape(-1, w_fine.shape[2])
    wide_b = w_coarse.reshape(-1, w_coarse.shape[2])
    feat_ext = with_halo(masked, "tile", HALO, 0)
    place_ext = with_halo(places, "tile", HALO, 1).astype(jnp.float32)
    places32 = places.astype(jnp.float32)
    top = points + 2 * HALO - 1

    nbr_f = nbr_fine[0].T
    fine_idx = jnp.where(
        nbr_f >= 0, jnp.clip(rows_here[:, None] + nbr_f, 0, top), -1
    )
    hidden = conv(feat_ext, place_ext, fine_idx, places32, kernel_points, wide_a, 256, True)
    hidden_ext = with_halo(hidden, "tile", HALO, 0)

    sub = jnp.clip(sub_index[0] - anchor, 0, points - 1)
    pick = (rows_here[:, None] == sub[None, :]).astype(jnp.bfloat16)
    centres = jnp.dot(places, pick, preferred_element_type=jnp.float32)
    nbr_c = nbr_coarse[0].T
    coarse_idx = jnp.where(nbr_c >= 0, jnp.clip(sub[:, None] + nbr_c, 0, top), -1)
    agg = conv(hidden_ext, place_ext, coarse_idx, centres, kernel_points, None, 256, False)

    coarse_out = lax.dot_general(
        wide_b, agg, (((0,), (1,)), ((), ())), preferred_element_type=jnp.float32
    ).astype(jnp.bfloat16)
    grad_part = lax.dot_general(
        agg, grad_out[0], (((0,), (1,)), ((), ())), preferred_element_type=jnp.float32
    )
    grad_total = lax.psum(grad_part, ("tile", "rep"))
    scale = 1.0 / math.sqrt(lax.axis_size("tile") * lax.axis_size("rep") * coarse)
    grad_wb = (grad_total * scale).reshape(w_coarse.shape)
    return (coarse_out[None], grad_wb)


def solution(mesh):
    placed = (
        P("rep", None, "tile"),
        P("rep", None, "tile"),
        P("rep", None, "tile"),
        P("rep", "tile"),
        P("rep", "tile"),
        P("rep", None, "tile"),
        P(),
        P(),
        P(),
        P("rep", None, "tile"),
    )
    return jax.shard_map(
        shards, mesh=mesh, in_specs=placed, out_specs=(P("rep", None, "tile"), P()), check_vma=False
    )
```

time: 914 us -> 312 us (0.34)
  local copies, waits for them, and re-layouts: 648 us -> 11.4 us
  Pallas kernels: 0 us -> 117 us
  matrix products: 48.1 us -> 3.48 us
  other arithmetic: 44 us -> 5.1 us
    gather x11 -> x0, local copies, waits for them, and re-layouts: 575 us -> none  [the longest x5 287 us: conv_block(): near_feat = jnp.take(source, local_rows, axis=1, mode='clip')]
    pallas_call x0 -> x2, Pallas kernels: none -> 117 us  [conv(): pl.pallas_call(functools.partial(conv_kernel, slots, kps, local, chunks,...]
    dot_general x11 -> x3, matrix products: 48.1 us -> 3.48 us  [the longest x1 2 us: shards(): lax.dot_general(agg, grad_out[0], (((0,), (1,)), ((), ())), preferred_ele...]
    convert_element_type x10 -> x0, local copies, waits for them, and re-layouts: 35.8 us -> none  [the longest x5 21.6 us: conv_block(): summed = jnp.einsum('kjb,cjb->kcb', weights, near_feat, preferred_element...]
    sub x6 -> x0, other arithmetic: 32.2 us -> none  [the longest x5 32.2 us: conv_block(): offsets = near_pos - centre[:, None, :]]
    sub x5 -> x0, local copies, waits for them, and re-layouts: 26.1 us -> none  [conv_block(): offsets = near_pos - centre[:, None, :]]
  transfers between devices with their start and end apart: 7 -> 7, of which waited for: 4 -> 2; matrix products, arithmetic and copies ran while one was open for 9% -> 3% of each run, Pallas kernels for 0% -> 0%
where the time goes in v1:
time: 312 us; the launch traced here: 309 us
  waiting for transfers between devices  138 us (44%)
  Pallas kernels  117 us (38%)
  starting transfers between devices  18.6 us (6%)
  between operations  15.2 us (5%)
  local copies, waits for them, and re-layouts  11.4 us (4%)
  other arithmetic  5.1 us (2%)
  matrix products  3.48 us (1%)
    psum x1, waiting for transfers between devices, shards(): grad_total = lax.psum(grad_part, ('tile', 'rep'))  138 us
    pallas_call x2, Pallas kernels, conv(): pl.pallas_call(functools.partial(conv_kernel, slots, kps, local, chunks,...  117 us
    ppermute x3, starting transfers between devices, with_halo(): lax.ppermute(tail, axis, [(i, (i + 1) % count) for i in range(ends)])  12.8 us
  transfers between devices with their start and end apart: 7, of which 2 were waited for; matrix products, arithmetic and copies ran while one was open for 3% of the time, Pallas kernels for 0%

profile of v1, /device:TPU:3, one launch (start us, length us, event | category | flops | bytes accessed | tf_op | source)
XLA Modules:
  0.0 308.7 jit_solution(9624416121122917252)
XLA Ops:
  7.2 0.0 copy-start
  7.2 0.0 all-reduce.2.cloned.1.call-start
  8.0 1.3 copy.22
  9.4 0.3 fusion.4
  9.7 0.0 copy-start.3
  9.7 0.8 copy-done.3
  10.5 0.7 fusion.17
  11.2 1.9 collective-permute-start.1
  13.2 4.3 %collective-permute-start = (bf16[512,128]{1,0:T(8,128)(2,1)}, bf16[512,128]{1,0:T(8,128)(2,1)}, u32[]{:S(2)}, u32[]{:S(2)}) collective-permute-start(bf16[512,128]{1,0:T(8,128)(2,1)} %get-tuple-element.10), channel_id=1, source_target_pairs={{0,2},{2,4},{4,6},{6,8},{8,10},{10,12},{12,14},{14,16},{16,18},{18... | collective-permute-start | bytes 393224 | tf_op jit(solution)/shard_map/ppermute | solution.py:26
  17.4 0.6 fusion.18
  18.0 1.9 collective-permute-start.3
  20.0 4.3 %collective-permute-start.2 = (bf16[3,512]{1,0:T(4,128)(2,1)}, bf16[3,512]{1,0:T(4,128)(2,1)S(1)}, u32[]{:S(2)}, u32[]{:S(2)}) collective-permute-start(bf16[3,512]{1,0:T(4,128)(2,1)} %get-tuple-element.14), channel_id=1, source_target_pairs={{0,2},{2,4},{4,6},{6,8},{8,10},{10,12},{12,14},{14,16},{16,18},{18... | collective-permute-start | bytes 9224 | tf_op jit(solution)/shard_map/ppermute | solution.py:26
  24.2 0.6 bitcast_convert_fusion
  24.8 0.1 fusion.8
  25.0 0.0 copy-done.9
  25.0 0.1 copy.18
  25.1 0.2 reshape.65.idx_s
  25.3 0.1 copy.19
  25.4 0.1 reshape.57.idx_v
  25.6 0.3 copy.20
  25.9 0.0 copy-start.7
  25.9 0.5 reshape.66.idx_s
  26.4 0.3 copy.21
  26.7 0.3 reshape.60.idx_v
  27.0 2.1 broadcast_in_dim.17
  29.2 2.5 reshape.61.cen
  31.7 0.0 collective-permute-done.3
  31.7 0.0 collective-permute-done.2
  31.7 0.0 collective-permute-done.1
  31.7 0.0 collective-permute-done
  31.7 1.0 pad_maximum_fusion.src
  32.8 91.5 %fine_conv.1 = bf16[2048,128]{1,0:T(8,128)(2,1)S(1)} custom-call(s32[8,1,8192]{2,1,0:T(1,128)S(1)} %reshape.66.idx_s, s32[256,256]{1,0:T(8,128)S(1)} %reshape.60.idx_v, f32[3,256,256]{2,1,0:T(8,128)S(1)} %reshape.61.cen, f32[3,15]{1,0:T(4,128)S(1)} %copy-done.2, bf16[3072,128]{1,0:T(8,128)(2,1)S(1)} %pad_maximum_fusion.src, ...), custom_call_target="tpu_custom_call" | custom-call | tf_op jit(solution)/shard_map/fine_conv/pallas_call | solution.py:156
  124.3 1.9 collective-permute-start.5
  126.2 4.3 %collective-permute-start.4 = (bf16[512,128]{1,0:T(8,128)(2,1)S(1)}, bf16[512,128]{1,0:T(8,128)(2,1)S(1)}, u32[]{:S(2)}, u32[]{:S(2)}) collective-permute-start(bf16[512,128]{1,0:T(8,128)(2,1)S(1)} %get-tuple-element.8), channel_id=1, source_target_pairs={{0,2},{2,4},{4,6},{6,8},{8,10},{10,12},{12,14},{14,16},{16,18},{18... | collective-permute-start | bytes 393224 | tf_op jit(solution)/shard_map/ppermute | solution.py:26
  130.5 0.8 fusion.3
  131.2 0.3 broadcast_in_dim.15
  131.5 0.2 reshape.58.cen
  131.7 0.0 copy-start.5
  131.8 0.0 collective-permute-done.5
  131.8 0.6 collective-permute-done.4
  132.4 0.1 pad_maximum_fusion.1.src
  132.4 25.1 %coarse_agg.1 = bf16[512,1920]{1,0:T(8,128)(2,1)S(1)} custom-call(s32[2,1,8192]{2,1,0:T(1,128)S(1)} %reshape.65.idx_s, s32[64,256]{1,0:T(8,128)S(1)} %reshape.57.idx_v, f32[3,64,256]{2,1,0:T(8,128)S(1)} %reshape.58.cen, f32[3,15]{1,0:T(4,128)S(1)} %copy-done.2, bf16[3072,128]{1,0:T(8,128)(2,1)S(1)} %pad_maximum_fusion.1.src, ...), custom_call_target="tpu_custom_call" | custom-call | tf_op jit(solution)/shard_map/coarse_agg/pallas_call | solution.py:156
  157.5 2.0 fusion.5
  159.5 0.0 all-reduce.2.cloned.1.call-update
  159.6 0.7 fusion.2
  160.3 0.8 copy.25
  161.1 137.8 %all-reduce.2.cloned.1.call-done = f32[1920,256]{1,0:T(8,128)} async-done(((f32[1920,256]{1,0:T(8,128)}), f32[1920,256]{1,0:T(8,128)}) %all-reduce.2.cloned.1.call-update) | async-done | bytes 1966096 | tf_op jit(solution)/shard_map/psum | solution.py:221
  298.9 2.9 broadcast_multiply_fusion
  (21 shorter events, 0.1 us)
Async XLA Ops:
  7.2 152.4 %copy-start = (bf16[15,128,256]{2,1,0:T(8,128)(2,1)S(1)}, bf16[15,128,256]{2,1,0:T(8,128)(2,1)}, u32[]{:S(2)}) copy-start(bf16[15,128,256]{2,1,0:T(8,128)(2,1)} %param.18) | copy-start | bytes 2949124
  7.2 10.3 %copy-start.8 = (bf16[1,3,2048]{2,1,0:T(4,128)(2,1)S(1)}, bf16[1,3,2048]{2,1,0:T(4,128)(2,1)}, u32[]{:S(2)}) copy-start(bf16[1,3,2048]{2,1,0:T(4,128)(2,1)} %param.11) | copy-start | bytes 36868
  7.2 17.6 %copy-start.6 = (s32[1,32,2048]{2,1,0:T(8,128)S(1)}, s32[1,32,2048]{2,1,0:T(8,128)}, u32[]{:S(2)}) copy-start(s32[1,32,2048]{2,1,0:T(8,128)} %param.12) | copy-start | bytes 786436
  7.2 17.7 %copy-start.10 = (s32[1,512]{1,0:T(1,128)S(1)}, s32[1,512]{1,0:T(1,128)}, u32[]{:S(2)}) copy-start(s32[1,512]{1,0:T(1,128)} %param.14) | copy-start | bytes 6148
  7.2 17.7 %copy-start.9 = (s32[1,32,512]{2,1,0:T(8,128)S(1)}, s32[1,32,512]{2,1,0:T(8,128)}, u32[]{:S(2)}) copy-start(s32[1,32,512]{2,1,0:T(8,128)} %param.15) | copy-start | bytes 196612
  7.2 291.7 %all-reduce.2.cloned.1.call-start = ((), (), s32[]{:S(2)}) async-start(), calls=%async_computation | async-start | bytes 3932160 | tf_op jit(solution)/shard_map/psum | solution.py:221
  9.7 0.8 copy-start.3
  11.2 20.5 %collective-permute-start.1 = (bf16[512,128]{1,0:T(8,128)(2,1)}, bf16[512,128]{1,0:T(8,128)(2,1)}, u32[]{:S(2)}, u32[]{:S(2)}) collective-permute-start(bf16[512,128]{1,0:T(8,128)(2,1)} %get-tuple-element.11), channel_id=1, source_target_pairs={{2,0},{4,2},{6,4},{8,6},{10,8},{12,10},{14,12},{16,14},{18,16},{20... | collective-permute-start | bytes 393224 | tf_op jit(solution)/shard_map/ppermute | solution.py:28
  13.2 18.6 %collective-permute-start = (bf16[512,128]{1,0:T(8,128)(2,1)}, bf16[512,128]{1,0:T(8,128)(2,1)}, u32[]{:S(2)}, u32[]{:S(2)}) collective-permute-start(bf16[512,128]{1,0:T(8,128)(2,1)} %get-tuple-element.10), channel_id=1, source_target_pairs={{0,2},{2,4},{4,6},{6,8},{8,10},{10,12},{12,14},{14,16},{16,18},{18... | collective-permute-start | bytes 393224 | tf_op jit(solution)/shard_map/ppermute | solution.py:26
  18.0 13.6 %collective-permute-start.3 = (bf16[3,512]{1,0:T(4,128)(2,1)}, bf16[3,512]{1,0:T(4,128)(2,1)S(1)}, u32[]{:S(2)}, u32[]{:S(2)}) collective-permute-start(bf16[3,512]{1,0:T(4,128)(2,1)} %get-tuple-element.15), channel_id=1, source_target_pairs={{2,0},{4,2},{6,4},{8,6},{10,8},{12,10},{14,12},{16,14},{18,16},{20... | collective-permute-start | bytes 9224 | tf_op jit(solution)/shard_map/ppermute | solution.py:28
  20.0 11.7 %collective-permute-start.2 = (bf16[3,512]{1,0:T(4,128)(2,1)}, bf16[3,512]{1,0:T(4,128)(2,1)S(1)}, u32[]{:S(2)}, u32[]{:S(2)}) collective-permute-start(bf16[3,512]{1,0:T(4,128)(2,1)} %get-tuple-element.14), channel_id=1, source_target_pairs={{0,2},{2,4},{4,6},{6,8},{8,10},{10,12},{12,14},{14,16},{16,18},{18... | collective-permute-start | bytes 9224 | tf_op jit(solution)/shard_map/ppermute | solution.py:26
  25.9 1.1 copy-start.7
  29.2 2.6 copy-start.4
  29.2 3.6 %copy-start.1 = (bf16[15,128,128]{2,1,0:T(8,128)(2,1)S(1)}, bf16[15,128,128]{2,1,0:T(8,128)(2,1)}, u32[]{:S(2)}) copy-start(bf16[15,128,128]{2,1,0:T(8,128)(2,1)} %param.17) | copy-start | bytes 1474564
  29.2 3.6 %copy-start.2 = (f32[3,15]{1,0:T(4,128)S(1)}, f32[3,15]{1,0:T(4,128)}, u32[]{:S(2)}) copy-start(f32[3,15]{1,0:T(4,128)} %kp.3) | copy-start | bytes 544
  124.3 7.5 %collective-permute-start.5 = (bf16[512,128]{1,0:T(8,128)(2,1)S(1)}, bf16[512,128]{1,0:T(8,128)(2,1)S(1)}, u32[]{:S(2)}, u32[]{:S(2)}) collective-permute-start(bf16[512,128]{1,0:T(8,128)(2,1)S(1)} %get-tuple-element.9), channel_id=1, source_target_pairs={{2,0},{4,2},{6,4},{8,6},{10,8},{12,10},{14,12},{16,14},{18,16},{20... | collective-permute-start | bytes 393224 | tf_op jit(solution)/shard_map/ppermute | solution.py:28
  126.2 6.2 %collective-permute-start.4 = (bf16[512,128]{1,0:T(8,128)(2,1)S(1)}, bf16[512,128]{1,0:T(8,128)(2,1)S(1)}, u32[]{:S(2)}, u32[]{:S(2)}) collective-permute-start(bf16[512,128]{1,0:T(8,128)(2,1)S(1)} %get-tuple-element.8), channel_id=1, source_target_pairs={{0,2},{2,4},{4,6},{6,8},{8,10},{10,12},{12,14},{14,16},{16,18},{18... | collective-permute-start | bytes 393224 | tf_op jit(solution)/shard_map/ppermute | solution.py:26
  131.7 25.8 %copy-start.5 = (bf16[1,256,512]{2,1,0:T(8,128)(2,1)S(1)}, bf16[1,256,512]{2,1,0:T(8,128)(2,1)}, u32[]{:S(2)}) copy-start(bf16[1,256,512]{2,1,0:T(8,128)(2,1)} %param.19) | copy-start | bytes 786436
Sparse Core Ops, SparseCore 0:
  159.7 139.2 all-reduce.1

commit v2 on v1

--- a/solution.py
+++ b/solution.py
@@ -16,19 +16,200 @@
 leak_slope = 0.1
 
 
-def with_halo(cells, axis, width, dim):
-    count = lax.axis_size(axis)
-    ends = count - 1
-    head = lax.slice_in_dim(cells, 0, width, axis=dim)
-    tail = lax.slice_in_dim(cells, cells.shape[dim] - width, cells.shape[dim], axis=dim)
-    return jnp.concatenate(
-        [
-            lax.ppermute(tail, axis, [(i, (i + 1) % count) for i in range(ends)]),
-            cells,
-            lax.ppermute(head, axis, [((i + 1) % count, i) for i in range(ends)]),
+def meet(partners):
+    barrier = pltpu.get_barrier_semaphore()
+    for partner in partners:
+        pl.semaphore_signal(
+            barrier, inc=1, device_id=partner, device_id_type=pl.DeviceIdType.MESH
+        )
+    pl.semaphore_wait(barrier, len(partners))
+
+
+def remote(src, dst, send_sem, recv_sem, partner):
+    return pltpu.make_async_remote_copy(
+        src_ref=src,
+        dst_ref=dst,
+        send_sem=send_sem,
+        recv_sem=recv_sem,
+        device_id=partner,
+        device_id_type=pl.DeviceIdType.MESH,
+    )
+
+
+def halo_kernel(tiles, dims, *refs):
+    n = len(dims)
+    ins, outs, (send_sem, recv_sem) = refs[:n], refs[n : 2 * n], refs[2 * n :]
+    me = lax.axis_index("tile")
+    left = {"tile": lax.rem(me + tiles - 1, tiles)}
+    right = {"tile": lax.rem(me + 1, tiles)}
+    meet((left, right))
+
+    def part(ref, dim, start, size):
+        return ref.at[pl.ds(start, size), :] if dim == 0 else ref.at[:, pl.ds(start, size)]
+
+    copies = []
+    for j, (src, dst, dim) in enumerate(zip(ins, outs, dims)):
+        size = src.shape[dim]
+        copies.append(
+            remote(
+                part(src, dim, size - HALO, HALO),
+                part(dst, dim, 0, HALO),
+                send_sem.at[2 * j],
+                recv_sem.at[2 * j],
+                right,
+            )
+        )
+        copies.append(
+            remote(
+                part(src, dim, 0, HALO),
+                part(dst, dim, size + HALO, HALO),
+                send_sem.at[2 * j + 1],
+                recv_sem.at[2 * j + 1],
+                left,
+            )
+        )
+    for copy in copies:
+        copy.start()
+    for src, dst, dim in zip(ins, outs, dims):
+        size = src.shape[dim]
+        if dim == 0:
+            dst[HALO : HALO + size, :] = src[...]
+        else:
+            dst[:, HALO : HALO + size] = src[...]
+    for copy in copies:
+        copy.wait()
+
+
+def with_halo(tiles, arrays, dims, collective_id):
+    shapes = []
+    for x, dim in zip(arrays, dims):
+        shape = list(x.shape)
+        shape[dim] += 2 * HALO
+        shapes.append(jax.ShapeDtypeStruct(tuple(shape), x.dtype))
+    whole = pl.BlockSpec(memory_space=pltpu.VMEM)
+    return pl.pallas_call(
+        functools.partial(halo_kernel, tiles, dims),
+        out_shape=tuple(shapes),
+        in_specs=[whole] * len(arrays),
+        out_specs=tuple([whole] * len(arrays)),
+        scratch_shapes=[
+            pltpu.SemaphoreType.DMA((2 * len(arrays),)),
+            pltpu.SemaphoreType.DMA((2 * len(arrays),)),
         ],
-        axis=dim,
-    )
+        compiler_params=pltpu.CompilerParams(
+            collective_id=collective_id,
+            has_side_effects=True,
+            vmem_limit_bytes=16 * 1024 * 1024,
+        ),
+        name="halo",
+    )(*arrays)
+
+
+def reduce_plan(tiles, rows):
+    halvings = 0
+    while 2 ** (halvings + 1) <= tiles and rows % 32 == 0:
+        rows //= 2
+        halvings += 1
+    return halvings, tiles.bit_length() - 1 - halvings
+
+
+def reduce_kernel(tiles, scale, part, out, *refs):
+    rows = part.shape[0]
+    half = part.shape[1] // 2
+    halvings, swaps = reduce_plan(tiles, rows)
+    steps = 1 + halvings + swaps
+    outbox, inbox = refs[:steps], refs[steps : 2 * steps]
+    acc, joined, other, send_sem, recv_sem = refs[2 * steps :]
+    me = lax.axis_index("tile")
+    rep = lax.axis_index("rep")
+    bits = [(me // 2**b) % 2 for b in range(halvings + swaps)]
+    peer = {"rep": 1 - rep}
+    partners = [{"tile": me + (1 - 2 * bit) * 2**b} for b, bit in enumerate(bits)]
+    meet([peer] + partners)
+
+    def trade(step, partner):
+        copy = remote(
+            outbox[step], inbox[step], send_sem.at[step], recv_sem.at[step], partner
+        )
+        copy.start()
+        return copy
+
+    own_cols = pl.ds(pl.multiple_of(rep * half, half), half)
+    other_cols = pl.ds(pl.multiple_of((1 - rep) * half, half), half)
+    outbox[0][...] = part[:, other_cols].astype(jnp.bfloat16)
+    trade(0, peer).wait()
+    acc[...] = part[:, own_cols] + inbox[0][...].astype(jnp.float32)
+
+    low, size = 0, rows
+    for b in range(halvings):
+        size //= 2
+        keep = pl.ds(pl.multiple_of(low + bits[b] * size, 16), size)
+        give = pl.ds(pl.multiple_of(low + (1 - bits[b]) * size, 16), size)
+        outbox[1 + b][...] = acc[give, :].astype(jnp.bfloat16)
+        trade(1 + b, partners[b]).wait()
+        acc[keep, :] += inbox[1 + b][...].astype(jnp.float32)
+        low = low + bits[b] * size
+    here = pl.ds(pl.multiple_of(low, 16), size)
+    total = acc[here, :]
+    for b in range(halvings, halvings + swaps):
+        outbox[1 + b][...] = total.astype(jnp.bfloat16)
+        trade(1 + b, partners[b]).wait()
+        total = outbox[1 + b][...].astype(jnp.float32) + inbox[1 + b][...].astype(jnp.float32)
+    joined[here, :] = total.astype(jnp.bfloat16)
+    for j, b in enumerate(reversed(range(halvings))):
+        here = pl.ds(pl.multiple_of(low, 16), size)
+        copy = remote(
+            joined.at[here, :],
+            joined.at[here, :],
+            send_sem.at[steps + j],
+            recv_sem.at[steps + j],
+            partners[b],
+        )
+        copy.start()
+        copy.wait()
+        low = low - bits[b] * size
+        size *= 2
+    copy = remote(
+        joined, other, send_sem.at[steps + halvings], recv_sem.at[steps + halvings], peer
+    )
+    copy.start()
+    out[:, own_cols] = joined[...].astype(jnp.float32) * scale
+    copy.wait()
+    out[:, other_cols] = other[...].astype(jnp.float32) * scale
+
+
+def reduce_grad(tiles, part, scale):
+    rows, cols = part.shape
+    half = cols // 2
+    halvings, swaps = reduce_plan(tiles, rows)
+    boxes = [(rows, half)]
+    size = rows
+    for b in range(halvings):
+        size //= 2
+        boxes.append((size, half))
+    boxes += [(size, half)] * swaps
+    boxes = [pltpu.VMEM(box, jnp.bfloat16) for box in boxes]
+    sems = len(boxes) + halvings + 1
+    whole = pl.BlockSpec(memory_space=pltpu.VMEM)
+    return pl.pallas_call(
+        functools.partial(reduce_kernel, tiles, scale),
+        out_shape=jax.ShapeDtypeStruct(part.shape, jnp.float32),
+        in_specs=[whole],
+        out_specs=whole,
+        scratch_shapes=boxes
+        + boxes
+        + [
+            pltpu.VMEM((rows, half), jnp.float32),
+            pltpu.VMEM((rows, half), jnp.bfloat16),
+            pltpu.VMEM((rows, half), jnp.bfloat16),
+            pltpu.SemaphoreType.DMA((sems,)),
+            pltpu.SemaphoreType.DMA((sems,)),
+        ],
+        compiler_params=pltpu.CompilerParams(
+            collective_id=2, has_side_effects=True, vmem_limit_bytes=24 * 1024 * 1024
+        ),
+        name="reduce_grad",
+    )(part)
 
 
 def conv_kernel(
@@ -193,9 +374,11 @@
     places = coords[0]
     wide_a = w_fine.reshape(-1, w_fine.shape[2])
     wide_b = w_coarse.reshape(-1, w_coarse.shape[2])
-    feat_ext = with_halo(masked, "tile", HALO, 0)
-    place_ext = with_halo(places, "tile", HALO, 1).astype(jnp.float32)
     places32 = places.astype(jnp.float32)
+    tiles = lax.axis_size("tile")
+    feat_ext, place_ext = with_halo(
+        tiles, (masked, jnp.pad(places32, ((0, 5), (0, 0)))), (0, 1), 0
+    )
     top = points + 2 * HALO - 1
 
     nbr_f = nbr_fine[0].T
@@ -203,7 +386,7 @@
         nbr_f >= 0, jnp.clip(rows_here[:, None] + nbr_f, 0, top), -1
     )
     hidden = conv(feat_ext, place_ext, fine_idx, places32, kernel_points, wide_a, 256, True)
-    hidden_ext = with_halo(hidden, "tile", HALO, 0)
+    (hidden_ext,) = with_halo(tiles, (hidden,), (0,), 1)
 
     sub = jnp.clip(sub_index[0] - anchor, 0, points - 1)
     pick = (rows_here[:, None] == sub[None, :]).astype(jnp.bfloat16)
@@ -218,9 +401,12 @@
     grad_part = lax.dot_general(
         agg, grad_out[0], (((0,), (1,)), ((), ())), preferred_element_type=jnp.float32
     )
-    grad_total = lax.psum(grad_part, ("tile", "rep"))
-    scale = 1.0 / math.sqrt(lax.axis_size("tile") * lax.axis_size("rep") * coarse)
-    grad_wb = (grad_total * scale).reshape(w_coarse.shape)
+    scale = 1.0 / math.sqrt(tiles * lax.axis_size("rep") * coarse)
+    if tiles & (tiles - 1) == 0 and lax.axis_size("rep") == 2:
+        grad_total = reduce_grad(tiles, grad_part, scale)
+    else:
+        grad_total = lax.psum(grad_part, ("tile", "rep")) * scale
+    grad_wb = grad_total.reshape(w_coarse.shape)
     return (coarse_out[None], grad_wb)
 
 

time: 312 us -> 197 us (0.63)
  waiting for transfers between devices: 138 us -> 0 us
  Pallas kernels: 117 us -> 173 us
  starting transfers between devices: 18.6 us -> 0 us
  between operations: 15.2 us -> 1.57 us
  local copies, waits for them, and re-layouts: 11.4 us -> 15.7 us
    psum x1 -> x0, waiting for transfers between devices: 138 us -> none  [shards(): grad_total = lax.psum(grad_part, ('tile', 'rep'))]
    pallas_call x0 -> x3, Pallas kernels: none -> 56.9 us  [the longest x1 37.8 us: reduce_grad(): pl.pallas_call(functools.partial(reduce_kernel, tiles, scale), out_shape=...]
    ppermute x6 -> x0, starting transfers between devices: 18.5 us -> none  [the longest x3 12.8 us: with_halo(): lax.ppermute(tail, axis, [(i, (i + 1) % count) for i in range(ends)])]
  transfers between devices with their start and end apart: 7 -> 0, of which waited for: 2 -> 0; matrix products, arithmetic and copies ran while one was open for 3% -> 0% of each run, Pallas kernels for 0% -> 0%
where the time goes in v2:
time: 197 us
  Pallas kernels  173 us (88%)
  local copies, waits for them, and re-layouts  15.7 us (8%)
  other arithmetic  3.1 us (2%)
  matrix products  2.9 us (1%)
    pallas_call x2, Pallas kernels, conv(): pl.pallas_call(functools.partial(conv_kernel, slots, kps, local, chunks,...  116 us
    pallas_call x1, Pallas kernels, reduce_grad(): pl.pallas_call(functools.partial(reduce_kernel, tiles, scale), out_shape=...  37.8 us
    pallas_call x2, Pallas kernels, with_halo(): pl.pallas_call(functools.partial(halo_kernel, tiles, dims), out_shape=tup...  19.2 us
    unnamed x15, local copies, waits for them, and re-layouts  4.25 us

profile of v2, /device:TPU:3, one launch (start us, length us, event | category | flops | bytes accessed | tf_op | source)
XLA Modules:
  0.0 196.6 jit_solution(1621986522275788995)
XLA Ops:
  0.6 0.0 copy-start
  0.6 0.8 subtract_clamp_fusion
  1.4 0.9 broadcast_maximum_fusion.1
  2.3 0.1 copy.18
  2.4 0.0 copy-start.4
  2.4 0.2 reshape.65.idx_s
  2.6 0.1 copy.19
  2.7 0.1 reshape.57.idx_v
  2.9 1.5 fusion.3
  4.3 0.3 broadcast_in_dim.15
  4.6 0.2 reshape.58.cen
  4.9 0.0 copy-done.4
  4.9 0.1 fusion.8
  5.0 1.3 copy.20
  6.3 0.0 copy-start.5
  6.3 1.7 reshape.66.idx_s
  8.0 1.3 copy.21
  9.3 1.5 reshape.60.idx_v
  10.8 0.0 copy-done.5
  10.8 2.1 %broadcast_in_dim.17 = f32[3,2048,32]{2,1,0:T(8,128)} broadcast(f32[3,2048]{1,0:T(4,128)S(1)} %bitcast_convert_fusion), dimensions={0,1} | broadcast | bytes 811008 | tf_op jit(solution)/shard_map/broadcast_in_dim | solution.py:321
  13.0 2.4 %reshape.61.cen = f32[3,256,256]{2,1,0:T(8,128)S(1)} reshape(f32[3,2048,32]{2,1,0:T(8,128)} %broadcast_in_dim.17) | data formatting | bytes 1572864 | tf_op jit(solution)/shard_map/reshape | solution.py:321
  15.4 0.0 copy-start.1
  15.4 0.0 copy-start.2
  15.4 2.1 %copy.22 = bf16[1,128,2048]{1,2,0:T(8,128)(2,1)} copy(bf16[1,128,2048]{2,1,0:T(8,128)(2,1)} %param.10) | data formatting | bytes 1048576 | tf_op args[0]
  18.2 1.4 fusion.4.refs_0_
  19.6 10.9 %halo.2 = (bf16[3072,128]{1,0:T(8,128)(2,1)S(1)}, f32[8,3072]{1,0:T(8,128)S(1)}) custom-call(bf16[2048,128]{1,0:T(8,128)(2,1)S(1)} %fusion.4.refs_0_, f32[8,2048]{1,0:T(8,128)S(1)} %pad.4.refs_1_), custom_call_target="tpu_custom_call" | custom-call | tf_op jit(solution)/shard_map/halo/pallas_call | solution.py:90
  30.5 0.0 copy-done.1
  30.5 0.0 copy-done.2
  30.5 91.4 %fine_conv.1.refs_0_ = bf16[2048,128]{1,0:T(8,128)(2,1)S(1)} custom-call(s32[8,1,8192]{2,1,0:T(1,128)S(1)} %reshape.66.idx_s, s32[256,256]{1,0:T(8,128)S(1)} %reshape.60.idx_v, f32[3,256,256]{2,1,0:T(8,128)S(1)} %reshape.61.cen, f32[3,15]{1,0:T(4,128)S(1)} %copy-done.2, bf16[3072,128]{1,0:T(8,128)(2,1)S(1)} %get-tuple-element.4.src, ...), custom_call_target="tpu_custom_call" | custom-call | tf_op jit(solution)/shard_map/fine_conv/pallas_call | solution.py:337
  121.9 8.3 %halo.3.src = bf16[3072,128]{1,0:T(8,128)(2,1)S(1)} custom-call(bf16[2048,128]{1,0:T(8,128)(2,1)S(1)} %fine_conv.1.refs_0_), custom_call_target="tpu_custom_call" | custom-call | tf_op jit(solution)/shard_map/halo/pallas_call | solution.py:90
  130.2 25.0 %coarse_agg.1 = bf16[512,1920]{1,0:T(8,128)(2,1)S(1)} custom-call(s32[2,1,8192]{2,1,0:T(1,128)S(1)} %reshape.65.idx_s, s32[64,256]{1,0:T(8,128)S(1)} %reshape.57.idx_v, f32[3,64,256]{2,1,0:T(8,128)S(1)} %reshape.58.cen, f32[3,15]{1,0:T(4,128)S(1)} %copy-done.2, bf16[3072,128]{1,0:T(8,128)(2,1)S(1)} %halo.3.src, f32[8,3072]{1,0:T(8,128)S(1)} %get-tuple-element.5.pos), custom_call_target="tpu_custom_call" | custom-call | tf_op jit(solution)/shard_map/coarse_agg/pallas_call | solution.py:337
  155.2 0.0 copy-done
  155.2 0.0 copy-start.3
  155.2 0.7 fusion.2
  156.0 0.8 copy.25
  156.8 0.0 copy-done.3
  156.8 0.7 fusion.5.part
  157.5 37.8 %reduce_grad.1 = f32[1920,256]{1,0:T(8,128)S(1)} custom-call(f32[1920,256]{1,0:T(8,128)S(1)} %fusion.5.part), custom_call_target="tpu_custom_call" | custom-call | tf_op jit(solution)/shard_map/reduce_grad/pallas_call | solution.py:194
  195.3 1.3 copy.28
  (3 shorter events, 0.0 us)
Async XLA Ops:
  0.6 154.6 %copy-start = (bf16[15,128,256]{2,1,0:T(8,128)(2,1)S(1)}, bf16[15,128,256]{2,1,0:T(8,128)(2,1)}, u32[]{:S(2)}) copy-start(bf16[15,128,256]{2,1,0:T(8,128)(2,1)} %param.18) | copy-start | bytes 2949124
  2.4 2.4 %copy-start.4 = (s32[1,32,2048]{2,1,0:T(8,128)S(1)}, s32[1,32,2048]{2,1,0:T(8,128)}, u32[]{:S(2)}) copy-start(s32[1,32,2048]{2,1,0:T(8,128)} %param.12) | copy-start | bytes 786436
  6.3 4.5 %copy-start.5 = (bf16[1,3,2048]{2,1,0:T(4,128)(2,1)S(1)}, bf16[1,3,2048]{2,1,0:T(4,128)(2,1)}, u32[]{:S(2)}) copy-start(bf16[1,3,2048]{2,1,0:T(4,128)(2,1)} %param.11) | copy-start | bytes 36868
  15.4 15.1 %copy-start.1 = (bf16[15,128,128]{2,1,0:T(8,128)(2,1)S(1)}, bf16[15,128,128]{2,1,0:T(8,128)(2,1)}, u32[]{:S(2)}) copy-start(bf16[15,128,128]{2,1,0:T(8,128)(2,1)} %param.17) | copy-start | bytes 1474564
  15.4 15.1 %copy-start.2 = (f32[3,15]{1,0:T(4,128)S(1)}, f32[3,15]{1,0:T(4,128)}, u32[]{:S(2)}) copy-start(f32[3,15]{1,0:T(4,128)} %kp.3) | copy-start | bytes 544
  155.2 1.6 copy-start.3

commit v3 on v2

--- a/solution.py
+++ b/solution.py
@@ -11,6 +11,7 @@
 HALO = 512
 GROUP = 8
 LANES = 128
+UNROLL = 8
 
 kernel_sigma = 2.0
 leak_slope = 0.1
@@ -227,9 +228,9 @@
     *rest,
 ):
     if last:
-        w, out, rows32, infl, g_even, g_odd, agg = rest
+        w, out, rows32, infl, gs, agg = rest
     else:
-        out, rows32, infl, g_even, g_odd, agg = rest
+        out, rows32, infl, gs, agg = rest
     step = pl.program_id(0)
     blocks = idx_v.shape[0]
     width = GROUP * slots
@@ -255,7 +256,20 @@
                 piece = jnp.broadcast_to(pos[d : d + 1, pl.ds(start, LANES)], idx.shape)
                 got = jnp.take_along_axis(piece, lane, axis=1)
                 near[d] = jnp.where(here, got, near[d])
-        offs = [near[d] - cen[d, :, cols] for d in range(3)]
+        point = (
+            lax.broadcasted_iota(jnp.int32, idx.shape, 0) * GROUP
+            + (lax.broadcasted_iota(jnp.int32, idx.shape, 1) + half * LANES) // slots
+        )
+        at_lane = jnp.bitwise_and(point, LANES - 1)
+        at_chunk = jnp.right_shift(point, 7)
+        offs = []
+        for d in range(3):
+            centre = jnp.zeros(idx.shape, jnp.float32)
+            for c in range(cen.shape[1] // LANES):
+                piece = jnp.broadcast_to(cen[d : d + 1, c * LANES : (c + 1) * LANES], idx.shape)
+                got = jnp.take_along_axis(piece, at_lane, axis=1)
+                centre = jnp.where(at_chunk == c, got, centre)
+            offs.append(near[d] - centre)
         present = idx >= 0
         for k in range(kps):
             a0 = offs[0] - kp[0, k]
@@ -274,31 +288,33 @@
 
     def fetch(block, g):
         base = block * width
-        for r in range(width):
-            row = idx_s[0, 0, base + r]
-            g[r : r + 1, :] = rows32[pl.ds(row, 1), :]
-
-    def combine(block, g):
+        for r in range(0, width, 8):
+            g[r : r + 8, :] = jnp.concatenate(
+                [rows32[pl.ds(idx_s[0, 0, base + r + q], 1), :] for q in range(8)], axis=0
+            )
+
+    def product(block, g):
         parts = []
         for k in range(kps + 1):
             one = jnp.broadcast_to(infl[k, pl.ds(block, 1), :], (GROUP, width))
             parts.append(jnp.where(own, one, 0.0))
         lhs = jnp.concatenate(parts, axis=0).astype(jnp.bfloat16)
-        res = jnp.dot(lhs, g[...].astype(jnp.bfloat16), preferred_element_type=jnp.float32)
+        return jnp.dot(lhs, g[...].astype(jnp.bfloat16), preferred_element_type=jnp.float32)
+
+    def put(block, res):
         at = pl.ds(pl.multiple_of(block * GROUP, GROUP), GROUP)
         for k in range(kps):
             agg[at, k * LANES : (k + 1) * LANES] = res[k * GROUP : (k + 1) * GROUP]
 
-    fetch(0, g_even)
-
-    def pair(p, carry):
-        fetch(2 * p + 1, g_odd)
-        combine(2 * p, g_even)
-        fetch(jnp.minimum(2 * p + 2, blocks - 1), g_even)
-        combine(2 * p + 1, g_odd)
+    def batch(p, carry):
+        for q in range(UNROLL):
+            fetch(UNROLL * p + q, gs.at[q])
+        res = [product(UNROLL * p + q, gs.at[q]) for q in range(UNROLL)]
+        for q in range(UNROLL):
+            put(UNROLL * p + q, res[q])
         return carry
 
-    lax.fori_loop(0, blocks // 2, pair, 0)
+    lax.fori_loop(0, blocks // UNROLL, batch, 0)
     flat = agg[...].astype(jnp.bfloat16)
     if last:
         pre = jnp.dot(flat, w[...], preferred_element_type=jnp.float32)
@@ -318,19 +334,18 @@
     width = GROUP * slots
     idx_s = jnp.maximum(local_idx, 0).reshape(steps, 1, per_step * slots)
     idx_v = local_idx.reshape(count // GROUP, width)
-    cen = jnp.broadcast_to(centres[:, :, None], (3, count, slots)).reshape(3, count // GROUP, width)
     chunks = (per_step + 2 * HALO) // LANES if local else total // LANES
     last = w is not None
     outs = w.shape[1] if last else kps * chans
     in_specs = [
         pl.BlockSpec((1, 1, per_step * slots), lambda i: (i, 0, 0), memory_space=pltpu.SMEM),
         pl.BlockSpec((blocks, width), lambda i: (i, 0)),
-        pl.BlockSpec((3, blocks, width), lambda i: (0, i, 0)),
+        pl.BlockSpec((3, per_step), lambda i: (0, i)),
         pl.BlockSpec(memory_space=pltpu.SMEM),
         pl.BlockSpec((total, chans), lambda i: (0, 0)),
         pl.BlockSpec(place_ext.shape, lambda i: (0, 0)),
     ]
-    args = [idx_s, idx_v, cen, kernel_points, rows, place_ext]
+    args = [idx_s, idx_v, centres, kernel_points, rows, place_ext]
     if last:
         in_specs.append(pl.BlockSpec(w.shape, lambda i: (0, 0)))
         args.append(w)
@@ -343,8 +358,7 @@
         scratch_shapes=[
             pltpu.VMEM((total, chans), jnp.float32),
             pltpu.VMEM((kps + 1, blocks, width), jnp.float32),
-            pltpu.VMEM((width, chans), jnp.float32),
-            pltpu.VMEM((width, chans), jnp.float32),
+            pltpu.VMEM((UNROLL, width, chans), jnp.float32),
             pltpu.VMEM((per_step, kps * chans), jnp.float32),
         ],
         compiler_params=pltpu.CompilerParams(vmem_limit_bytes=40 * 1024 * 1024),

time: 197 us -> 166 us (0.84)
  Pallas kernels: 173 us -> 148 us
  local copies, waits for them, and re-layouts: 15.7 us -> 9.48 us
    pallas_call x2, Pallas kernels: 116 us -> 91.5 us  [conv(): pl.pallas_call(functools.partial(conv_kernel, slots, kps, local, chunks,...]
    reshape x2 -> x0, local copies, waits for them, and re-layouts: 2.64 us -> none  [conv(): jnp.broadcast_to(centres[:, :, None], (3, count, slots))]
    broadcast_in_dim x2 -> x0, local copies, waits for them, and re-layouts: 2.38 us -> none  [conv(): jnp.broadcast_to(centres[:, :, None], (3, count, slots))]
where the time goes in v3:
time: 166 us; the launch traced here: 165 us
  Pallas kernels  148 us (89%)
  local copies, waits for them, and re-layouts  9.48 us (6%)
  matrix products  2.9 us (2%)
  other arithmetic  2.7 us (2%)
    pallas_call x2, Pallas kernels, conv(): pl.pallas_call(functools.partial(conv_kernel, slots, kps, local, chunks,...  91.5 us
    pallas_call x1, Pallas kernels, reduce_grad(): pl.pallas_call(functools.partial(reduce_kernel, tiles, scale), out_shape=...  37.8 us
    pallas_call x2, Pallas kernels, with_halo(): pl.pallas_call(functools.partial(halo_kernel, tiles, dims), out_shape=tup...  19.2 us

profile of v3, /device:TPU:3, one launch (start us, length us, event | category | flops | bytes accessed | tf_op | source)
XLA Modules:
  0.0 165.1 jit_solution(10717733754270001559)
XLA Ops:
  0.6 0.0 copy-start
  0.6 0.0 copy-start.3
  1.5 0.4 copy-done
  1.9 0.7 subtract_clamp_fusion
  2.5 1.5 fusion.3.cen
  4.0 0.7 bitcast_convert_fusion.cen
  4.8 0.9 broadcast_maximum_fusion.1
  5.6 0.0 copy-start.5
  5.6 0.1 copy.18
  5.8 0.2 reshape.51.idx_s
  5.9 0.1 copy.19
  6.1 0.1 reshape.45.idx_v
  6.2 0.0 copy-done.3
  6.2 0.3 copy.22
  6.5 0.3 fusion.4.refs_0_
  6.9 10.9 %halo.2 = (bf16[3072,128]{1,0:T(8,128)(2,1)S(1)}, f32[8,3072]{1,0:T(8,128)S(1)}) custom-call(bf16[2048,128]{1,0:T(8,128)(2,1)S(1)} %fusion.4.refs_0_, f32[8,2048]{1,0:T(8,128)S(1)} %pad.4.refs_1_), custom_call_target="tpu_custom_call" | custom-call | tf_op jit(solution)/shard_map/halo/pallas_call | solution.py:91
  17.7 0.0 copy-done.5
  17.7 0.1 fusion.8
  17.8 1.3 copy.21
  19.1 0.0 copy-start.1
  19.1 0.0 copy-start.2
  19.1 1.6 reshape.47.idx_v
  20.7 1.3 copy.20
  22.0 1.7 %reshape.52.idx_s = s32[8,1,8192]{2,1,0:T(1,128)S(1)} reshape(s32[2048,32]{1,0:T(8,128)} %copy.20) | data formatting | bytes 524288 | tf_op jit(solution)/shard_map/reshape | solution.py:335
  23.7 0.0 copy-done.1
  23.7 0.0 copy-done.2
  23.7 71.5 %fine_conv.1.refs_0_ = bf16[2048,128]{1,0:T(8,128)(2,1)S(1)} custom-call(s32[8,1,8192]{2,1,0:T(1,128)S(1)} %reshape.52.idx_s, s32[256,256]{1,0:T(8,128)S(1)} %reshape.47.idx_v, f32[3,2048]{1,0:T(4,128)S(1)} %bitcast_convert_fusion.cen, f32[3,15]{1,0:T(4,128)S(1)} %copy-done.2, bf16[3072,128]{1,0:T(8,128)(2,1)S(1)} %get-tuple-element.4.src, ...), custom_call_target="tpu_custom_call" | custom-call | tf_op jit(solution)/shard_map/fine_conv/pallas_call | solution.py:352
  95.2 8.3 %halo.3.src = bf16[3072,128]{1,0:T(8,128)(2,1)S(1)} custom-call(bf16[2048,128]{1,0:T(8,128)(2,1)S(1)} %fine_conv.1.refs_0_), custom_call_target="tpu_custom_call" | custom-call | tf_op jit(solution)/shard_map/halo/pallas_call | solution.py:91
  103.5 20.0 %coarse_agg.1 = bf16[512,1920]{1,0:T(8,128)(2,1)S(1)} custom-call(s32[2,1,8192]{2,1,0:T(1,128)S(1)} %reshape.51.idx_s, s32[64,256]{1,0:T(8,128)S(1)} %reshape.45.idx_v, f32[3,512]{1,0:T(4,128)S(1)} %fusion.3.cen, f32[3,15]{1,0:T(4,128)S(1)} %copy-done.2, bf16[3072,128]{1,0:T(8,128)(2,1)S(1)} %halo.3.src, f32[8,3072]{1,0:T(8,128)S(1)} %get-tuple-element.5.pos), custom_call_target="tpu_custom_call" | custom-call | tf_op jit(solution)/shard_map/coarse_agg/pallas_call | solution.py:352
  123.6 0.0 copy-start.4
  123.6 0.7 fusion.2
  124.3 0.2 copy-done.4
  124.5 0.7 fusion.5.part
  125.3 37.8 %reduce_grad.1 = f32[1920,256]{1,0:T(8,128)S(1)} custom-call(f32[1920,256]{1,0:T(8,128)S(1)} %fusion.5.part), custom_call_target="tpu_custom_call" | custom-call | tf_op jit(solution)/shard_map/reduce_grad/pallas_call | solution.py:195
  163.0 0.8 copy.25
  163.9 1.3 copy.28
  (2 shorter events, 0.0 us)
Async XLA Ops:
  0.6 1.2 copy-start
  0.6 5.6 %copy-start.3 = (bf16[1,128,2048]{2,1,0:T(8,128)(2,1)S(1)}, bf16[1,128,2048]{2,1,0:T(8,128)(2,1)}, u32[]{:S(2)}) copy-start(bf16[1,128,2048]{2,1,0:T(8,128)(2,1)} %param.10) | copy-start | bytes 1572868
  5.6 12.1 %copy-start.5 = (s32[1,32,2048]{2,1,0:T(8,128)S(1)}, s32[1,32,2048]{2,1,0:T(8,128)}, u32[]{:S(2)}) copy-start(s32[1,32,2048]{2,1,0:T(8,128)} %param.12) | copy-start | bytes 786436
  19.1 4.6 %copy-start.1 = (bf16[15,128,128]{2,1,0:T(8,128)(2,1)S(1)}, bf16[15,128,128]{2,1,0:T(8,128)(2,1)}, u32[]{:S(2)}) copy-start(bf16[15,128,128]{2,1,0:T(8,128)(2,1)} %param.17) | copy-start | bytes 1474564
  19.1 4.6 %copy-start.2 = (f32[3,15]{1,0:T(4,128)S(1)}, f32[3,15]{1,0:T(4,128)}, u32[]{:S(2)}) copy-start(f32[3,15]{1,0:T(4,128)} %kp.3) | copy-start | bytes 544
  123.6 1.0 copy-start.4

commit v4 on v3

--- a/solution.py
+++ b/solution.py
@@ -137,12 +137,33 @@
 
     own_cols = pl.ds(pl.multiple_of(rep * half, half), half)
     other_cols = pl.ds(pl.multiple_of((1 - rep) * half, half), half)
-    outbox[0][...] = part[:, other_cols].astype(jnp.bfloat16)
-    trade(0, peer).wait()
-    acc[...] = part[:, own_cols] + inbox[0][...].astype(jnp.float32)
-
-    low, size = 0, rows
-    for b in range(halvings):
+    low, size = 0, rows // 2
+    keep = pl.ds(pl.multiple_of(bits[0] * size, 16), size)
+    give = pl.ds(pl.multiple_of((1 - bits[0]) * size, 16), size)
+    extra = steps + 2 * halvings + 1
+    firsts = []
+    for piece, sem in ((give, 0), (keep, extra)):
+        outbox[0][piece, :] = part[piece, other_cols].astype(jnp.bfloat16)
+        copy = remote(
+            outbox[0].at[piece, :],
+            inbox[0].at[piece, :],
+            send_sem.at[sem],
+            recv_sem.at[sem],
+            peer,
+        )
+        copy.start()
+        firsts.append(copy)
+    firsts[0].wait()
+    outbox[1][...] = (
+        part[give, own_cols] + inbox[0][give, :].astype(jnp.float32)
+    ).astype(jnp.bfloat16)
+    second = trade(1, partners[0])
+    firsts[1].wait()
+    acc[keep, :] = part[keep, own_cols] + inbox[0][keep, :].astype(jnp.float32)
+    second.wait()
+    acc[keep, :] += inbox[1][...].astype(jnp.float32)
+    low = bits[0] * size
+    for b in range(1, halvings):
         size //= 2
         keep = pl.ds(pl.multiple_of(low + bits[b] * size, 16), size)
         give = pl.ds(pl.multiple_of(low + (1 - bits[b]) * size, 16), size)
@@ -157,6 +178,20 @@
         trade(1 + b, partners[b]).wait()
         total = outbox[1 + b][...].astype(jnp.float32) + inbox[1 + b][...].astype(jnp.float32)
     joined[here, :] = total.astype(jnp.bfloat16)
+    forwards = []
+
+    def forward(region):
+        sem = steps + halvings + len(forwards)
+        copy = remote(
+            joined.at[region, :],
+            other.at[region, :],
+            send_sem.at[sem],
+            recv_sem.at[sem],
+            peer,
+        )
+        copy.start()
+        forwards.append(copy)
+
     for j, b in enumerate(reversed(range(halvings))):
         here = pl.ds(pl.multiple_of(low, 16), size)
         copy = remote(
@@ -167,15 +202,15 @@
             partners[b],
         )
         copy.start()
+        if j == 0:
+            forward(here)
         copy.wait()
+        forward(pl.ds(pl.multiple_of(low + (1 - 2 * bits[b]) * size, 16), size))
         low = low - bits[b] * size
         size *= 2
-    copy = remote(
-        joined, other, send_sem.at[steps + halvings], recv_sem.at[steps + halvings], peer
-    )
-    copy.start()
     out[:, own_cols] = joined[...].astype(jnp.float32) * scale
-    copy.wait()
+    for copy in forwards:
+        copy.wait()
     out[:, other_cols] = other[...].astype(jnp.float32) * scale
 
 
@@ -190,7 +225,7 @@
         boxes.append((size, half))
     boxes += [(size, half)] * swaps
     boxes = [pltpu.VMEM(box, jnp.bfloat16) for box in boxes]
-    sems = len(boxes) + halvings + 1
+    sems = len(boxes) + 2 * halvings + 2
     whole = pl.BlockSpec(memory_space=pltpu.VMEM)
     return pl.pallas_call(
         functools.partial(reduce_kernel, tiles, scale),

time: 166 us -> 165 us (level)
  no operation moved by 1% of the time
where the time goes in v4:
time: 165 us
  Pallas kernels  148 us (90%)
  local copies, waits for them, and re-layouts  9.48 us (6%)
  matrix products  2.9 us (2%)
  other arithmetic  2.7 us (2%)
    pallas_call x2, Pallas kernels, conv(): pl.pallas_call(functools.partial(conv_kernel, slots, kps, local, chunks,...  91.5 us
    pallas_call x1, Pallas kernels, reduce_grad(): pl.pallas_call(functools.partial(reduce_kernel, tiles, scale), out_shape=...  37.2 us
    pallas_call x2, Pallas kernels, with_halo(): pl.pallas_call(functools.partial(halo_kernel, tiles, dims), out_shape=tup...  19.2 us

profile of v4, /device:TPU:3, one launch (start us, length us, event | category | flops | bytes accessed | tf_op | source)
XLA Modules:
  0.0 164.5 jit_solution(15499478732508324440)
XLA Ops:
  0.6 0.0 copy-start
  0.6 0.0 copy-start.3
  1.5 0.4 copy-done
  1.9 0.7 subtract_clamp_fusion
  2.5 1.5 fusion.3.cen
  4.0 0.7 bitcast_convert_fusion.cen
  4.8 0.9 broadcast_maximum_fusion.1
  5.6 0.0 copy-start.5
  5.6 0.1 copy.18
  5.8 0.2 reshape.51.idx_s
  5.9 0.1 copy.19
  6.1 0.1 reshape.45.idx_v
  6.2 0.0 copy-done.3
  6.2 0.3 copy.22
  6.5 0.3 fusion.4.refs_0_
  6.9 10.9 %halo.2 = (bf16[3072,128]{1,0:T(8,128)(2,1)S(1)}, f32[8,3072]{1,0:T(8,128)S(1)}) custom-call(bf16[2048,128]{1,0:T(8,128)(2,1)S(1)} %fusion.4.refs_0_, f32[8,2048]{1,0:T(8,128)S(1)} %pad.4.refs_1_), custom_call_target="tpu_custom_call" | custom-call | tf_op jit(solution)/shard_map/halo/pallas_call | solution.py:91
  17.7 0.0 copy-done.5
  17.7 0.1 fusion.8
  17.8 1.3 copy.21
  19.1 0.0 copy-start.1
  19.1 0.0 copy-start.2
  19.1 1.6 reshape.47.idx_v
  20.7 1.3 copy.20
  22.0 1.7 %reshape.52.idx_s = s32[8,1,8192]{2,1,0:T(1,128)S(1)} reshape(s32[2048,32]{1,0:T(8,128)} %copy.20) | data formatting | bytes 524288 | tf_op jit(solution)/shard_map/reshape | solution.py:370
  23.7 0.0 copy-done.1
  23.7 0.0 copy-done.2
  23.7 71.5 %fine_conv.1.refs_0_ = bf16[2048,128]{1,0:T(8,128)(2,1)S(1)} custom-call(s32[8,1,8192]{2,1,0:T(1,128)S(1)} %reshape.52.idx_s, s32[256,256]{1,0:T(8,128)S(1)} %reshape.47.idx_v, f32[3,2048]{1,0:T(4,128)S(1)} %bitcast_convert_fusion.cen, f32[3,15]{1,0:T(4,128)S(1)} %copy-done.2, bf16[3072,128]{1,0:T(8,128)(2,1)S(1)} %get-tuple-element.4.src, ...), custom_call_target="tpu_custom_call" | custom-call | tf_op jit(solution)/shard_map/fine_conv/pallas_call | solution.py:387
  95.2 8.3 %halo.3.src = bf16[3072,128]{1,0:T(8,128)(2,1)S(1)} custom-call(bf16[2048,128]{1,0:T(8,128)(2,1)S(1)} %fine_conv.1.refs_0_), custom_call_target="tpu_custom_call" | custom-call | tf_op jit(solution)/shard_map/halo/pallas_call | solution.py:91
  103.5 20.1 %coarse_agg.1 = bf16[512,1920]{1,0:T(8,128)(2,1)S(1)} custom-call(s32[2,1,8192]{2,1,0:T(1,128)S(1)} %reshape.51.idx_s, s32[64,256]{1,0:T(8,128)S(1)} %reshape.45.idx_v, f32[3,512]{1,0:T(4,128)S(1)} %fusion.3.cen, f32[3,15]{1,0:T(4,128)S(1)} %copy-done.2, bf16[3072,128]{1,0:T(8,128)(2,1)S(1)} %halo.3.src, f32[8,3072]{1,0:T(8,128)S(1)} %get-tuple-element.5.pos), custom_call_target="tpu_custom_call" | custom-call | tf_op jit(solution)/shard_map/coarse_agg/pallas_call | solution.py:387
  123.6 0.0 copy-start.4
  123.6 0.7 fusion.2
  124.3 0.2 copy-done.4
  124.5 0.7 fusion.5.part
  125.2 37.2 %reduce_grad.1 = f32[1920,256]{1,0:T(8,128)S(1)} custom-call(f32[1920,256]{1,0:T(8,128)S(1)} %fusion.5.part), custom_call_target="tpu_custom_call" | custom-call | tf_op jit(solution)/shard_map/reduce_grad/pallas_call | solution.py:230
  162.4 0.8 copy.25
  163.3 1.3 copy.28
  (2 shorter events, 0.0 us)
Async XLA Ops:
  0.6 1.2 copy-start
  0.6 5.6 %copy-start.3 = (bf16[1,128,2048]{2,1,0:T(8,128)(2,1)S(1)}, bf16[1,128,2048]{2,1,0:T(8,128)(2,1)}, u32[]{:S(2)}) copy-start(bf16[1,128,2048]{2,1,0:T(8,128)(2,1)} %param.10) | copy-start | bytes 1572868
  5.6 12.1 %copy-start.5 = (s32[1,32,2048]{2,1,0:T(8,128)S(1)}, s32[1,32,2048]{2,1,0:T(8,128)}, u32[]{:S(2)}) copy-start(s32[1,32,2048]{2,1,0:T(8,128)} %param.12) | copy-start | bytes 786436
  19.1 4.6 %copy-start.1 = (bf16[15,128,128]{2,1,0:T(8,128)(2,1)S(1)}, bf16[15,128,128]{2,1,0:T(8,128)(2,1)}, u32[]{:S(2)}) copy-start(bf16[15,128,128]{2,1,0:T(8,128)(2,1)} %param.17) | copy-start | bytes 1474564
  19.1 4.6 %copy-start.2 = (f32[3,15]{1,0:T(4,128)S(1)}, f32[3,15]{1,0:T(4,128)}, u32[]{:S(2)}) copy-start(f32[3,15]{1,0:T(4,128)} %kp.3) | copy-start | bytes 544
  123.6 1.0 copy-start.4
